TPU v7x, 256 devices: a whole 4x4x8 slice. The times are simulated.
256 devices in a mesh: row: 16 (over x, y_hi, core), col: 16 (over z, y_lo).
Axes of the slice: x: 4, y: 4 (y_hi: 2, y_lo: 2; y = y_hi * 2 + y_lo), z: 8, core: 2. Of those that a mesh axis runs over, the one named last changes fastest.
Arguments:
- activations: bfloat16 [1024, 8192], P(None, 'row'), may hold values from -10 to 10
- cotangents: bfloat16 [1024, 8192], P(None, 'row'), may hold values from -10 to 10
- act_factor: bfloat16 [8192, 8192], P('row', 'col'), may hold values from -0.5 to 1.5
- grad_factor: bfloat16 [8192, 8192], P('row', 'col'), may hold values from -0.5 to 1.5
Outputs:
- act_updated: bfloat16 [8192, 8192], P('row', 'col')
- grad_updated: bfloat16 [8192, 8192], P('row', 'col')
All inputs are finite; a program needn't handle non-finite values.
Results may differ from a plain program's by a relative error of at most 0.0057.
Values may be sent and summed in bfloat16 or wider, within the bound.
No kernel may reach another device: no remote copies, remote signals or barrier semaphores. Data moves between devices by JAX's collectives and lax.ppermute only.
A program may use at most 64 MiB of HBM per device.

v0:
```python
import jax
import jax.numpy as jnp
from jax import lax
from jax.sharding import PartitionSpec as P

D = 8192
TOKENS = 1024
keep_scale = 1.45
gram_scale = 0.5


def times_transposed(factor_block, projected):
    return lax.dot_general(
        factor_block, projected, (((1,), (1,)), ((), ())), preferred_element_type=jnp.float32
    )


def local(activations, cotangents, act_factor, grad_factor):
    width = act_factor.shape[1]
    own_rows = lax.psum_scatter(
        jnp.concatenate(
            [
                jnp.dot(activations, act_factor, preferred_element_type=jnp.float32),
                jnp.dot(cotangents, grad_factor, preferred_element_type=jnp.float32),
            ],
            axis=1,
        ),
        "row",
        scatter_dimension=0,
        tiled=True,
    ).astype(jnp.bfloat16)
    projected = lax.all_gather(own_rows, "row", axis=0, tiled=True)
    squares = jnp.square(own_rows.astype(jnp.float32))
    act_total, grad_total = lax.psum(
        (jnp.sum(squares[:, :width]), jnp.sum(squares[:, width:])), ("row", "col")
    )
    act_mean = act_total / (TOKENS * D)
    grad_mean = grad_total / (TOKENS * D)
    act_proj = projected[:, :width]
    grad_proj = projected[:, width:]
    act_image, grad_image = lax.psum(
        (times_transposed(act_factor, act_proj), times_transposed(grad_factor, grad_proj)), "col"
    )
    act_image = act_image.astype(jnp.bfloat16)
    grad_image = grad_image.astype(jnp.bfloat16)
    act_change = jnp.dot(act_image, act_proj, preferred_element_type=jnp.float32)
    grad_change = jnp.dot(grad_image, grad_proj, preferred_element_type=jnp.float32)
    act_updated = (
        keep_scale * act_factor.astype(jnp.float32) - gram_scale * grad_mean / TOKENS * act_change
    ).astype(jnp.bfloat16)
    grad_updated = (
        keep_scale * grad_factor.astype(jnp.float32) - gram_scale * act_mean / TOKENS * grad_change
    ).astype(jnp.bfloat16)
    return (act_updated, grad_updated)


def solution(mesh):
    return jax.shard_map(
        local,
        mesh=mesh,
        in_specs=(P(None, "row"), P(None, "row"), P("row", "col"), P("row", "col")),
        out_specs=(P("row", "col"), P("row", "col")),
        check_vma=False,
    )
```

profile of v0, /device:TPU:16, one launch (start us, length us, event | category | flops | bytes accessed | tf_op | source)
XLA Modules:
  0.0 387.5 jit_solution(4529226681538673235)
XLA Ops:
  7.2 0.0 copy-start
  7.2 0.0 copy-start.3
  7.2 0.0 copy-start.5
  7.2 0.0 reduce-scatter.4.cloned.1.call-start
  7.2 1.1 copy-done
  8.4 1.8 fusion.10
  10.2 0.0 copy-done.3
  10.2 0.0 copy-done.5
  10.2 0.8 fusion.11
  11.0 2.5 pad_maximum_fusion
  13.5 5.3 %copy.7 = f32[1024,1024]{1,0:T(8,128)} copy(f32[1024,1024]{0,1:T(8,128)} %pad_maximum_fusion) | data formatting | bytes 8388608
  18.8 0.0 reduce-scatter.4.cloned.1.call-update
  18.8 0.0 all-gather.2.cloned.1.call-start
  18.9 89.7 %reduce-scatter.4.cloned.1.call-done = f32[64,1024]{1,0:T(8,128)} async-done(((f32[1024,1024]{1,0:T(8,128)}), f32[64,1024]{1,0:T(8,128)}) %reduce-scatter.4.cloned.1.call-update) | async-done | bytes 262160
  108.6 1.1 copy.8
  109.7 0.8 copy.6
  110.5 0.0 all-gather.2.cloned.1.call-update
  110.6 0.7 slice_reduce_fusion
  111.3 75.7 %all-reduce = (f32[]{:T(128)}, f32[]{:T(128)}) all-reduce(f32[]{:T(128)} %get-tuple-element.3, f32[]{:T(128)} %get-tuple-element.2), channel_id=1, replica_groups=mesh['row'=16,'col'=16] {'row','col'}, use_global_device_ids=true, to_apply=%region_2.0 | all-reduce | flops 2 | bytes 16 | tf_op jit(solution)/shard_map/psum | solution.py:34
  188.2 0.0 all-gather.2.cloned.1.call-done
  188.2 0.0 copy-start.1
  188.2 2.2 convolution_bitcast_fusion
  190.5 0.0 copy-done.1
  190.5 3.1 convolution_bitcast_fusion.1
  193.6 182.2 %all-reduce.3 = (bf16[512,1024]{0,1:T(8,128)(2,1)}, bf16[512,1024]{0,1:T(8,128)(2,1)}) all-reduce(f32[512,1024]{0,1:T(8,128)} %convolution_bitcast_fusion.1, f32[512,1024]{0,1:T(8,128)S(1)} %convolution_bitcast_fusion), channel_id=1, replica_groups=mesh['row'=16,'col'=16] {'col'}, use_global_device_ids=true, to_apply=%region_3.0 | all-reduce | flops 1048576 | bytes 6291456 | tf_op jit(solution)/shard_map/psum | solution.py:41
  375.8 0.0 copy-start.2
  375.8 0.0 copy-start.4
  375.8 3.4 fusion.2
  379.1 0.0 copy-done.2
  379.1 0.0 copy-done.4
  379.1 0.0 copy-done.6
  379.1 1.5 fusion.3
  (2 shorter events, 0.0 us)
Async XLA Ops:
  7.2 1.2 copy-start
  7.2 3.0 copy-start.3
  7.2 3.0 copy-start.5
  7.2 101.4 %reduce-scatter.4.cloned.1.call-start = ((), (), s32[]{:S(2)}) async-start(), calls=%async_computation.2 | async-start | bytes 4456448
  18.8 169.4 %all-gather.2.cloned.1.call-start = ((), (), s32[]{:S(2)}) async-start(), calls=%async_computation.1 | async-start | bytes 2228224 | tf_op jit(solution)/shard_map/all_gather | solution.py:32
  188.2 2.3 copy-start.1
  375.8 3.4 copy-start.2
  375.8 3.4 copy-start.4
  375.8 3.4 copy-start.6
Sparse Core Ops, SparseCore 0:
  19.0 89.6 reduce-scatter.3
  112.2 51.1 all-gather.1
where the time goes:
time: 388 us
  blocking collectives  258 us (66%)
  waiting for transfers between devices  89.8 us (23%)
  between operations  15.3 us (4%)
  matrix products  12.8 us (3%)
  local copies, waits for them, and re-layouts  8.43 us (2%)
    psum x1, blocking collectives, local(): lax.psum((times_transposed(act_factor, act_proj), times_transposed(grad_f...  182 us
    unnamed x3, waiting for transfers between devices  89.8 us
    psum x1, blocking collectives, local(): lax.psum((jnp.sum(squares[:, :width]), jnp.sum(squares[:, width:])), ('ro...  75.7 us
  transfers between devices with their start and end apart: 2, of which 1 were waited for; matrix products, arithmetic and copies ran while one was open for 0% of the time, Pallas kernels for 0%

commit v1 on v0

--- a/solution.py
+++ b/solution.py
@@ -32,7 +32,7 @@
     projected = lax.all_gather(own_rows, "row", axis=0, tiled=True)
     squares = jnp.square(own_rows.astype(jnp.float32))
     act_total, grad_total = lax.psum(
-        (jnp.sum(squares[:, :width]), jnp.sum(squares[:, width:])), ("row", "col")
+        lax.psum((jnp.sum(squares[:, :width]), jnp.sum(squares[:, width:])), "row"), "col"
     )
     act_mean = act_total / (TOKENS * D)
     grad_mean = grad_total / (TOKENS * D)

time: 388 us -> 369 us (0.951)
  blocking collectives: 258 us -> 213 us
  waiting for transfers between devices: 89.8 us -> 112 us
    psum x1, blocking collectives: 75.7 us -> 30 us  [local(): lax.psum((jnp.sum(squares[:, :width]), jnp.sum(squares[:, width:])), 'row')]
    all_gather x1, waiting for transfers between devices: 0.02 us -> 22.1 us  [local(): projected = lax.all_gather(own_rows, 'row', axis=0, tiled=True)]
  transfers between devices with their start and end apart: 2 -> 2, of which waited for: 1 -> 2; matrix products, arithmetic and copies ran while one was open for 0% -> 0% of each run, Pallas kernels for 0% -> 0%
where the time goes in v1:
time: 369 us; the launch traced here: 365 us
  blocking collectives  213 us (58%)
  waiting for transfers between devices  112 us (30%)
  between operations  15.4 us (4%)
  matrix products  12.8 us (3%)
  local copies, waits for them, and re-layouts  8.44 us (2%)
    psum x1, blocking collectives, local(): lax.psum((times_transposed(act_factor, act_proj), times_transposed(grad_f...  183 us
    unnamed x3, waiting for transfers between devices  89.8 us
    psum x1, blocking collectives, local(): lax.psum((jnp.sum(squares[:, :width]), jnp.sum(squares[:, width:])), 'row')  30 us
    all_gather x1, waiting for transfers between devices, local(): projected = lax.all_gather(own_rows, 'row', axis=0, tiled=True)  22.1 us
    unnamed x16, local copies, waits for them, and re-layouts  7.65 us
  transfers between devices with their start and end apart: 2, of which 2 were waited for; matrix products, arithmetic and copies ran while one was open for 0% of the time, Pallas kernels for 0%

profile of v1, /device:TPU:16, one launch (start us, length us, event | category | flops | bytes accessed | tf_op | source)
XLA Modules:
  0.0 365.1 jit_solution(6173727388618705415)
XLA Ops:
  7.2 0.0 copy-start
  7.2 0.0 copy-start.3
  7.2 0.0 copy-start.5
  7.2 0.0 reduce-scatter.4.cloned.1.call-start
  7.2 1.1 copy-done
  8.4 1.8 fusion.10
  10.2 0.0 copy-done.3
  10.2 0.0 copy-done.5
  10.2 0.8 fusion.11
  11.0 2.5 pad_maximum_fusion
  13.5 5.3 %copy.7 = f32[1024,1024]{1,0:T(8,128)} copy(f32[1024,1024]{0,1:T(8,128)} %pad_maximum_fusion) | data formatting | bytes 8388608
  18.8 0.0 reduce-scatter.4.cloned.1.call-update
  18.8 0.0 all-gather.2.cloned.1.call-start
  18.9 89.7 %reduce-scatter.4.cloned.1.call-done = f32[64,1024]{1,0:T(8,128)} async-done(((f32[1024,1024]{1,0:T(8,128)}), f32[64,1024]{1,0:T(8,128)}) %reduce-scatter.4.cloned.1.call-update) | async-done | bytes 262160
  108.6 1.1 copy.8
  109.7 0.8 copy.6
  110.5 0.0 all-gather.2.cloned.1.call-update
  110.6 0.7 slice_reduce_fusion
  111.3 30.0 %all-reduce.1 = (f32[]{:T(128)}, f32[]{:T(128)}) all-reduce(f32[]{:T(128)} %get-tuple-element.3, f32[]{:T(128)} %get-tuple-element.2), channel_id=1, replica_groups=mesh['row'=16,'col'=16] {'row'}, use_global_device_ids=true, to_apply=%region_2.0 | all-reduce | flops 2 | bytes 16 | tf_op jit(solution)/shard_map/psum | solution.py:35
  141.3 22.1 %all-gather.2.cloned.1.call-done = bf16[1024,1024]{1,0:T(8,128)(2,1)} async-done(((bf16[64,1024]{1,0:T(8,128)(2,1)}), bf16[1024,1024]{1,0:T(8,128)(2,1)}) %all-gather.2.cloned.1.call-update) | async-done | bytes 2097168 | tf_op jit(solution)/shard_map/all_gather | solution.py:32
  163.4 2.2 convolution_bitcast_fusion
  165.6 0.0 copy-done.1
  165.6 3.1 convolution_bitcast_fusion.1
  168.7 183.3 %all-reduce.3 = (bf16[512,1024]{0,1:T(8,128)(2,1)}, f32[]{:T(128)}, bf16[512,1024]{0,1:T(8,128)(2,1)}, f32[]{:T(128)}) all-reduce(f32[512,1024]{0,1:T(8,128)} %convolution_bitcast_fusion.1, f32[]{:T(128)} %get-tuple-element.8, f32[512,1024]{0,1:T(8,128)S(1)} %convolution_bitcast_fusion, ...), channel_id=1, replica_groups=mesh['row'=16,'col'=16] {'col'}, use_global_device_ids=true, to_apply=%region_4.0 | all-reduce | flops 1048578 | bytes 6291472 | tf_op jit(solution)/shard_map/psum | solution.py:41
  353.3 0.0 copy-start.2
  353.3 0.0 copy-start.4
  353.3 0.0 copy-start.6
  353.3 3.4 fusion.2
  356.7 0.0 copy-done.2
  356.7 0.0 copy-done.4
  356.7 0.0 copy-done.6
  356.7 1.5 fusion.3
  (2 shorter events, 0.0 us)
Async XLA Ops:
  7.2 1.2 copy-start
  7.2 3.0 copy-start.3
  7.2 3.0 copy-start.5
  7.2 101.4 %reduce-scatter.4.cloned.1.call-start = ((), (), s32[]{:S(2)}) async-start(), calls=%async_computation.2 | async-start | bytes 4456448
  18.8 144.6 %all-gather.2.cloned.1.call-start = ((), (), s32[]{:S(2)}) async-start(), calls=%async_computation.1 | async-start | bytes 2228224 | tf_op jit(solution)/shard_map/all_gather | solution.py:32
  163.4 2.2 copy-start.1
  353.3 3.4 copy-start.2
  353.3 3.4 copy-start.4
  353.3 3.4 copy-start.6
Sparse Core Ops, SparseCore 0:
  19.0 89.6 reduce-scatter.3
  112.2 51.0 all-gather.1
